TPU v7x, 512 devices: a whole 4x4x16 slice. The times are simulated.
512 devices in a mesh: term: 32 (over y, x, core), sector: 16 (over z).
Axes of the slice: x: 4, y: 4, z: 16, core: 2. Of those that a mesh axis runs over, the one named last changes fastest.
Arguments:
- wavefunction: bfloat16 [96, 256, 256], P('sector')
- left_operator_blocks: bfloat16 [384, 256, 256], P('term'), may hold values from -0.01953125 to 0.01953125
- right_operator_blocks: bfloat16 [384, 256, 256], P('term'), may hold values from -0.375 to 0.375
- fetch_index: int32 [32, 16, 16], P('term', 'sector'), may hold values from 0 to 5, as said below
- owner_link: int32 [384, 96], P('term', 'sector'), may hold values from 0 to 15, as said below
- lower_roots: bfloat16 [4, 96, 256, 256], P(None, 'sector', 'term')
- level_shift: float32 [4], replicated, may hold values from 0.5 to 2
Outputs:
- sigma: float32 [96, 256, 256], P('sector', 'term')
- correlations: float32 [4], replicated
Inputs may be any that keep to these rules, and one draw needn't show every extreme that they name: `fetch_index`: entry p of every list is a position within the 6 sectors of sector index p. `owner_link`: within the 12 x 6 entries that one device holds, every sector index occurs at least once.
All inputs are finite; a program needn't handle non-finite values.
Results may differ from a plain program's by a relative error of at most 0.0059.
Values may be sent and summed in bfloat16 or wider, within the bound.
A program may use at most 64 MiB of HBM per device.

v0:
```python
import jax
import jax.numpy as jnp
from jax import lax
from jax.sharding import PartitionSpec as P


def per_device(
    wavefunction,
    left_operator_blocks,
    right_operator_blocks,
    fetch_index,
    owner_link,
    lower_roots,
    level_shift,
):
    sec_dev = wavefunction.shape[0]
    block_width = wavefunction.shape[1]
    group_count = fetch_index.shape[2]
    own_requests = fetch_index.reshape(group_count, 1)
    store = lax.all_gather(wavefunction, "sector", axis=0, tiled=True)
    lookup = owner_link * sec_dev + own_requests[:, 0][owner_link]

    def one_sector(column):
        input_sectors = store[column]
        partial_contraction = jnp.einsum(
            "lhm,lmp->lhp", left_operator_blocks, input_sectors, preferred_element_type=jnp.float32
        ).astype(jnp.bfloat16)
        return jnp.einsum(
            "yxz,ysz->xs",
            partial_contraction,
            right_operator_blocks,
            preferred_element_type=jnp.float32,
        )

    partial_value = lax.map(one_sector, jnp.transpose(lookup))
    reduced = lax.psum_scatter(partial_value, "term", scatter_dimension=1, tiled=True)
    row_count = reduced.shape[1]
    row_start = lax.axis_index("term") * row_count
    psi_rows = lax.dynamic_slice_in_dim(wavefunction, row_start, row_count, 1)
    local_correlation = jnp.einsum(
        "ksab,sab->k", lower_roots, psi_rows, preferred_element_type=jnp.float32
    )
    total_cells = lax.axis_size("sector") * sec_dev * block_width * block_width
    correlations = lax.psum(local_correlation, ("term", "sector")) / total_cells
    sigma = reduced + jnp.einsum(
        "k,ksab->sab", level_shift * correlations, lower_roots.astype(jnp.float32)
    )
    return (sigma, correlations)


def solution(mesh):
    return jax.shard_map(
        per_device,
        mesh=mesh,
        in_specs=(
            P("sector", None, None),
            P("term", None, None),
            P("term", None, None),
            P("term", "sector", None),
            P("term", "sector"),
            P(None, "sector", "term", None),
            P(),
        ),
        out_specs=(P("sector", "term", None), P()),
        check_vma=False,
    )
```

profile of v0, /device:TPU:1, one launch (start us, length us, event | category | flops | bytes accessed | tf_op | source)
XLA Modules:
  0.0 328.3 jit_solution(2077307641894323809)
XLA Ops:
  7.2 0.7 all-gather.2.cloned.1.call-update
  8.0 0.8 copy.17
  8.8 0.7 compare_select_fusion.1
  9.4 0.1 copy.18
  9.7 1.2 gather_fusion.1
  11.1 152.4 %all-gather.2.cloned.1.call-done = bf16[96,256,256]{2,1,0:T(8,128)(2,1)} async-done(((bf16[6,256,256]{2,1,0:T(8,128)(2,1)}), bf16[96,256,256]{2,1,0:T(8,128)(2,1)}) %all-gather.2.cloned.1.call-update) | async-done | bytes 12582928 | tf_op jit(solution)/shard_map/all_gather | solution.py:20
  163.5 52.1 %while.10 = (s32[]{:T(128)}, f32[6,256,256]{2,1,0:T(8,128)}, s32[6,12]{1,0:T(8,128)S(1)}, bf16[96,256,256]{2,1,0:T(8,128)(2,1)}, bf16[12,256,256]{2,1,0:T(8,128)...) while((s32[]{:T(128)}, f32[6,256,256]{2,1,0:T(8,128)}, s32[6,12]{1,0:T(8,128)S(1)}, ...), condition=%wide.region_1.2_spmd, body=%wide.region_0.1_spmd.sunk | while | flops 806093888 | bytes 8130845 | solution.py:35
  163.5 5.2 %gather_fusion = bf16[12,256,256]{2,1,0:T(8,128)(2,1)S(1)} fusion(bf16[96,256,256]{2,1,0:T(8,128)(2,1)} %get-tuple-element.119, s32[1024]{0:T(1024)S(1)} %pad_clamp_fusion.3), kind=kCustom, calls=%fused_computation.clone.1 | custom fusion | bytes 3145776 | tf_op jit(solution)/shard_map/while/body/eval_jaxpr/gather | solution.py:24
  168.8 3.4 %fusion.27 = f32[6,256,256]{2,1,0:T(8,128)} fusion(f32[6,256,256]{2,1,0:T(8,128)} %get-tuple-element.110, s32[]{:T(128)S(6)} %copy.38, bf16[12,256,256]{2,1,0:T(8,128)(2,1)} %get-tuple-element.121, bf16[12,256,256]{2,1,0:T(8,128)(2,1)S(1)} %gather_fusion, bf16[12,256,256]{2,1,0:T(8,128)(2,1)S(1)} %get-tuple-element.120), kind=kOutput, calls=%fused_computation.6.clone.1 | convolution fusion | flops 806092800 | bytes 4980740 | tf_op jit(solution)/shard_map/while/body/eval_jaxpr/yxz,ysz->xs/dot_general | solution.py:28
  172.2 5.2 %gather_fusion = bf16[12,256,256]{2,1,0:T(8,128)(2,1)S(1)} fusion(bf16[96,256,256]{2,1,0:T(8,128)(2,1)} %get-tuple-element.119, s32[1024]{0:T(1024)S(1)} %pad_clamp_fusion.3), kind=kCustom, calls=%fused_computation.clone.1 | custom fusion | bytes 3145776 | tf_op jit(solution)/shard_map/while/body/eval_jaxpr/gather | solution.py:24
  177.4 3.5 %fusion.27 = f32[6,256,256]{2,1,0:T(8,128)} fusion(f32[6,256,256]{2,1,0:T(8,128)} %get-tuple-element.110, s32[]{:T(128)S(6)} %copy.38, bf16[12,256,256]{2,1,0:T(8,128)(2,1)} %get-tuple-element.121, bf16[12,256,256]{2,1,0:T(8,128)(2,1)S(1)} %gather_fusion, bf16[12,256,256]{2,1,0:T(8,128)(2,1)S(1)} %get-tuple-element.120), kind=kOutput, calls=%fused_computation.6.clone.1 | convolution fusion | flops 806092800 | bytes 4980740 | tf_op jit(solution)/shard_map/while/body/eval_jaxpr/yxz,ysz->xs/dot_general | solution.py:28
  180.9 5.2 %gather_fusion = bf16[12,256,256]{2,1,0:T(8,128)(2,1)S(1)} fusion(bf16[96,256,256]{2,1,0:T(8,128)(2,1)} %get-tuple-element.119, s32[1024]{0:T(1024)S(1)} %pad_clamp_fusion.3), kind=kCustom, calls=%fused_computation.clone.1 | custom fusion | bytes 3145776 | tf_op jit(solution)/shard_map/while/body/eval_jaxpr/gather | solution.py:24
  186.1 3.4 %fusion.27 = f32[6,256,256]{2,1,0:T(8,128)} fusion(f32[6,256,256]{2,1,0:T(8,128)} %get-tuple-element.110, s32[]{:T(128)S(6)} %copy.38, bf16[12,256,256]{2,1,0:T(8,128)(2,1)} %get-tuple-element.121, bf16[12,256,256]{2,1,0:T(8,128)(2,1)S(1)} %gather_fusion, bf16[12,256,256]{2,1,0:T(8,128)(2,1)S(1)} %get-tuple-element.120), kind=kOutput, calls=%fused_computation.6.clone.1 | convolution fusion | flops 806092800 | bytes 4980740 | tf_op jit(solution)/shard_map/while/body/eval_jaxpr/yxz,ysz->xs/dot_general | solution.py:28
  189.6 5.2 %gather_fusion = bf16[12,256,256]{2,1,0:T(8,128)(2,1)S(1)} fusion(bf16[96,256,256]{2,1,0:T(8,128)(2,1)} %get-tuple-element.119, s32[1024]{0:T(1024)S(1)} %pad_clamp_fusion.3), kind=kCustom, calls=%fused_computation.clone.1 | custom fusion | bytes 3145776 | tf_op jit(solution)/shard_map/while/body/eval_jaxpr/gather | solution.py:24
  194.8 3.4 %fusion.27 = f32[6,256,256]{2,1,0:T(8,128)} fusion(f32[6,256,256]{2,1,0:T(8,128)} %get-tuple-element.110, s32[]{:T(128)S(6)} %copy.38, bf16[12,256,256]{2,1,0:T(8,128)(2,1)} %get-tuple-element.121, bf16[12,256,256]{2,1,0:T(8,128)(2,1)S(1)} %gather_fusion, bf16[12,256,256]{2,1,0:T(8,128)(2,1)S(1)} %get-tuple-element.120), kind=kOutput, calls=%fused_computation.6.clone.1 | convolution fusion | flops 806092800 | bytes 4980740 | tf_op jit(solution)/shard_map/while/body/eval_jaxpr/yxz,ysz->xs/dot_general | solution.py:28
  198.3 5.2 %gather_fusion = bf16[12,256,256]{2,1,0:T(8,128)(2,1)S(1)} fusion(bf16[96,256,256]{2,1,0:T(8,128)(2,1)} %get-tuple-element.119, s32[1024]{0:T(1024)S(1)} %pad_clamp_fusion.3), kind=kCustom, calls=%fused_computation.clone.1 | custom fusion | bytes 3145776 | tf_op jit(solution)/shard_map/while/body/eval_jaxpr/gather | solution.py:24
  203.5 3.4 %fusion.27 = f32[6,256,256]{2,1,0:T(8,128)} fusion(f32[6,256,256]{2,1,0:T(8,128)} %get-tuple-element.110, s32[]{:T(128)S(6)} %copy.38, bf16[12,256,256]{2,1,0:T(8,128)(2,1)} %get-tuple-element.121, bf16[12,256,256]{2,1,0:T(8,128)(2,1)S(1)} %gather_fusion, bf16[12,256,256]{2,1,0:T(8,128)(2,1)S(1)} %get-tuple-element.120), kind=kOutput, calls=%fused_computation.6.clone.1 | convolution fusion | flops 806092800 | bytes 4980740 | tf_op jit(solution)/shard_map/while/body/eval_jaxpr/yxz,ysz->xs/dot_general | solution.py:28
  206.9 5.2 %gather_fusion = bf16[12,256,256]{2,1,0:T(8,128)(2,1)S(1)} fusion(bf16[96,256,256]{2,1,0:T(8,128)(2,1)} %get-tuple-element.119, s32[1024]{0:T(1024)S(1)} %pad_clamp_fusion.3), kind=kCustom, calls=%fused_computation.clone.1 | custom fusion | bytes 3145776 | tf_op jit(solution)/shard_map/while/body/eval_jaxpr/gather | solution.py:24
  212.2 3.4 %fusion.27 = f32[6,256,256]{2,1,0:T(8,128)} fusion(f32[6,256,256]{2,1,0:T(8,128)} %get-tuple-element.110, s32[]{:T(128)S(6)} %copy.38, bf16[12,256,256]{2,1,0:T(8,128)(2,1)} %get-tuple-element.121, bf16[12,256,256]{2,1,0:T(8,128)(2,1)S(1)} %gather_fusion, bf16[12,256,256]{2,1,0:T(8,128)(2,1)S(1)} %get-tuple-element.120), kind=kOutput, calls=%fused_computation.6.clone.1 | convolution fusion | flops 806092800 | bytes 4980740 | tf_op jit(solution)/shard_map/while/body/eval_jaxpr/yxz,ysz->xs/dot_general | solution.py:28
  215.6 0.7 dynamic-slice_bitcast_fusion
  216.4 0.3 convolution_bitcast_fusion
  216.6 103.1 %psum.7 = f32[4]{0:T(128)S(1)} all-reduce(f32[4]{0:T(128)S(1)} %convolution_bitcast_fusion), channel_id=1, replica_groups=mesh['term'=32,'sector'=16] {'term','sector'}, use_global_device_ids=true, to_apply=%region_3.4 | all-reduce | flops 4 | bytes 32 | tf_op jit(solution)/shard_map/psum | solution.py:44
  319.8 0.2 fusion.9
  320.0 1.4 bitcast_add_fusion
  (33 shorter events, 0.5 us)
Async XLA Ops:
  7.2 209.2 %copy-start = (bf16[4,6,8,256]{3,2,1,0:T(8,128)(2,1)S(1)}, bf16[4,6,8,256]{3,2,1,0:T(8,128)(2,1)}, u32[]{:S(2)}) copy-start(bf16[4,6,8,256]{3,2,1,0:T(8,128)(2,1)} %param.14) | copy-start | bytes 294916
  7.2 2.5 copy-start.1
  7.2 156.3 %all-gather.2.cloned.1.call-start = ((), (), s32[]{:S(2)}) async-start(), calls=%async_computation.1 | async-start | bytes 13369344 | tf_op jit(solution)/shard_map/all_gather | solution.py:20
  7.9 312.1 %reduce-scatter.2.cloned.1.call-start = ((), (), s32[]{:S(2)}) async-start(), calls=%async_computation.2 | async-start | bytes 1622016 | tf_op jit(solution)/shard_map/reduce_scatter | solution.py:36
  9.7 153.9 %copy-start.2 = (bf16[12,256,256]{2,1,0:T(8,128)(2,1)S(1)}, bf16[12,256,256]{2,1,0:T(8,128)(2,1)}, u32[]{:S(2)}) copy-start(bf16[12,256,256]{2,1,0:T(8,128)(2,1)} %param.10) | copy-start | bytes 4718596
  215.6 104.2 %copy-start.3 = (f32[4]{0:T(128)S(1)}, f32[4]{0:T(128)}, u32[]{:S(2)}) copy-start(f32[4]{0:T(128)} %param.15) | copy-start | bytes 52
  319.8 1.6 copy-start.4
Sparse Core Ops, SparseCore 0:
  10.1 153.3 all-gather.1
  215.8 97.6 reduce-scatter.1
where the time goes:
time: 329 us; the launch traced here: 328 us
  waiting for transfers between devices  153 us (47%)
  blocking collectives  103 us (31%)
  local copies, waits for them, and re-layouts  34.5 us (10%)
  matrix products  21 us (6%)
  between operations  14.1 us (4%)
    all_gather x1, waiting for transfers between devices, per_device(): store = lax.all_gather(wavefunction, 'sector', axis=0, tiled=True)  152 us
    psum x1, blocking collectives, per_device(): correlations = lax.psum(local_correlation, ('term', 'sector')) / total_cells  103 us
    gather x6, local copies, waits for them, and re-layouts, one_sector(): input_sectors = store[column]  31.3 us
    dot_general x6, matrix products, one_sector(): jnp.einsum('yxz,ysz->xs', partial_contraction, right_operator_blocks, pre...  20.6 us
  transfers between devices with their start and end apart: 2, of which 1 were waited for; matrix products, arithmetic and copies ran while one was open for 1% of the time, Pallas kernels for 0%

commit v1 on v0

--- a/solution.py
+++ b/solution.py
@@ -41,7 +41,9 @@
         "ksab,sab->k", lower_roots, psi_rows, preferred_element_type=jnp.float32
     )
     total_cells = lax.axis_size("sector") * sec_dev * block_width * block_width
-    correlations = lax.psum(local_correlation, ("term", "sector")) / total_cells
+    correlations = (
+        jnp.sum(lax.all_gather(local_correlation, ("term", "sector")), axis=0) / total_cells
+    )
     sigma = reduced + jnp.einsum(
         "k,ksab->sab", level_shift * correlations, lower_roots.astype(jnp.float32)
     )

time: 329 us -> 330 us (level)
    unnamed x0 -> x1, blocking collectives: none -> 103 us
    psum x1 -> x0, blocking collectives: 103 us -> none  [per_device(): correlations = lax.psum(local_correlation, ('term', 'sector')) / total_cells]
where the time goes in v1:
time: 330 us; the launch traced here: 329 us
  waiting for transfers between devices  153 us (46%)
  blocking collectives  103 us (31%)
  local copies, waits for them, and re-layouts  34.9 us (11%)
  matrix products  21 us (6%)
  between operations  14.1 us (4%)
    all_gather x1, waiting for transfers between devices, per_device(): store = lax.all_gather(wavefunction, 'sector', axis=0, tiled=True)  152 us
    unnamed x1, blocking collectives  103 us
    gather x6, local copies, waits for them, and re-layouts, one_sector(): input_sectors = store[column]  31.3 us
    dot_general x6, matrix products, one_sector(): jnp.einsum('yxz,ysz->xs', partial_contraction, right_operator_blocks, pre...  20.6 us
  transfers between devices with their start and end apart: 2, of which 1 were waited for; matrix products, arithmetic and copies ran while one was open for 1% of the time, Pallas kernels for 0%

profile of v1, /device:TPU:1, one launch (start us, length us, event | category | flops | bytes accessed | tf_op | source)
XLA Modules:
  0.0 328.9 jit_solution(9994035775407411090)
XLA Ops:
  7.2 0.7 all-gather.3.cloned.1.call-update
  8.0 0.8 copy.17
  8.8 0.7 compare_select_fusion.1
  9.7 1.2 gather_fusion.1
  11.1 152.4 %all-gather.3.cloned.1.call-done = bf16[96,256,256]{2,1,0:T(8,128)(2,1)} async-done(((bf16[6,256,256]{2,1,0:T(8,128)(2,1)}), bf16[96,256,256]{2,1,0:T(8,128)(2,1)}) %all-gather.3.cloned.1.call-update) | async-done | bytes 12582928 | tf_op jit(solution)/shard_map/all_gather | solution.py:20
  163.5 52.1 %while.10 = (s32[]{:T(128)}, f32[6,256,256]{2,1,0:T(8,128)}, s32[6,12]{1,0:T(8,128)S(1)}, bf16[96,256,256]{2,1,0:T(8,128)(2,1)}, bf16[12,256,256]{2,1,0:T(8,128)...) while((s32[]{:T(128)}, f32[6,256,256]{2,1,0:T(8,128)}, s32[6,12]{1,0:T(8,128)S(1)}, ...), condition=%wide.region_1.2_spmd, body=%wide.region_0.1_spmd.sunk | while | flops 806093888 | bytes 8130845 | solution.py:35
  163.5 5.2 %gather_fusion = bf16[12,256,256]{2,1,0:T(8,128)(2,1)S(1)} fusion(bf16[96,256,256]{2,1,0:T(8,128)(2,1)} %get-tuple-element.119, s32[1024]{0:T(1024)S(1)} %pad_clamp_fusion.3), kind=kCustom, calls=%fused_computation.clone.1 | custom fusion | bytes 3145776 | tf_op jit(solution)/shard_map/while/body/eval_jaxpr/gather | solution.py:24
  168.8 3.4 %fusion.27 = f32[6,256,256]{2,1,0:T(8,128)} fusion(f32[6,256,256]{2,1,0:T(8,128)} %get-tuple-element.110, s32[]{:T(128)S(6)} %copy.38, bf16[12,256,256]{2,1,0:T(8,128)(2,1)} %get-tuple-element.121, bf16[12,256,256]{2,1,0:T(8,128)(2,1)S(1)} %gather_fusion, bf16[12,256,256]{2,1,0:T(8,128)(2,1)S(1)} %get-tuple-element.120), kind=kOutput, calls=%fused_computation.6.clone.1 | convolution fusion | flops 806092800 | bytes 4980740 | tf_op jit(solution)/shard_map/while/body/eval_jaxpr/yxz,ysz->xs/dot_general | solution.py:28
  172.2 5.2 %gather_fusion = bf16[12,256,256]{2,1,0:T(8,128)(2,1)S(1)} fusion(bf16[96,256,256]{2,1,0:T(8,128)(2,1)} %get-tuple-element.119, s32[1024]{0:T(1024)S(1)} %pad_clamp_fusion.3), kind=kCustom, calls=%fused_computation.clone.1 | custom fusion | bytes 3145776 | tf_op jit(solution)/shard_map/while/body/eval_jaxpr/gather | solution.py:24
  177.4 3.4 %fusion.27 = f32[6,256,256]{2,1,0:T(8,128)} fusion(f32[6,256,256]{2,1,0:T(8,128)} %get-tuple-element.110, s32[]{:T(128)S(6)} %copy.38, bf16[12,256,256]{2,1,0:T(8,128)(2,1)} %get-tuple-element.121, bf16[12,256,256]{2,1,0:T(8,128)(2,1)S(1)} %gather_fusion, bf16[12,256,256]{2,1,0:T(8,128)(2,1)S(1)} %get-tuple-element.120), kind=kOutput, calls=%fused_computation.6.clone.1 | convolution fusion | flops 806092800 | bytes 4980740 | tf_op jit(solution)/shard_map/while/body/eval_jaxpr/yxz,ysz->xs/dot_general | solution.py:28
  180.9 5.2 %gather_fusion = bf16[12,256,256]{2,1,0:T(8,128)(2,1)S(1)} fusion(bf16[96,256,256]{2,1,0:T(8,128)(2,1)} %get-tuple-element.119, s32[1024]{0:T(1024)S(1)} %pad_clamp_fusion.3), kind=kCustom, calls=%fused_computation.clone.1 | custom fusion | bytes 3145776 | tf_op jit(solution)/shard_map/while/body/eval_jaxpr/gather | solution.py:24
  186.1 3.4 %fusion.27 = f32[6,256,256]{2,1,0:T(8,128)} fusion(f32[6,256,256]{2,1,0:T(8,128)} %get-tuple-element.110, s32[]{:T(128)S(6)} %copy.38, bf16[12,256,256]{2,1,0:T(8,128)(2,1)} %get-tuple-element.121, bf16[12,256,256]{2,1,0:T(8,128)(2,1)S(1)} %gather_fusion, bf16[12,256,256]{2,1,0:T(8,128)(2,1)S(1)} %get-tuple-element.120), kind=kOutput, calls=%fused_computation.6.clone.1 | convolution fusion | flops 806092800 | bytes 4980740 | tf_op jit(solution)/shard_map/while/body/eval_jaxpr/yxz,ysz->xs/dot_general | solution.py:28
  189.6 5.2 %gather_fusion = bf16[12,256,256]{2,1,0:T(8,128)(2,1)S(1)} fusion(bf16[96,256,256]{2,1,0:T(8,128)(2,1)} %get-tuple-element.119, s32[1024]{0:T(1024)S(1)} %pad_clamp_fusion.3), kind=kCustom, calls=%fused_computation.clone.1 | custom fusion | bytes 3145776 | tf_op jit(solution)/shard_map/while/body/eval_jaxpr/gather | solution.py:24
  194.8 3.4 %fusion.27 = f32[6,256,256]{2,1,0:T(8,128)} fusion(f32[6,256,256]{2,1,0:T(8,128)} %get-tuple-element.110, s32[]{:T(128)S(6)} %copy.38, bf16[12,256,256]{2,1,0:T(8,128)(2,1)} %get-tuple-element.121, bf16[12,256,256]{2,1,0:T(8,128)(2,1)S(1)} %gather_fusion, bf16[12,256,256]{2,1,0:T(8,128)(2,1)S(1)} %get-tuple-element.120), kind=kOutput, calls=%fused_computation.6.clone.1 | convolution fusion | flops 806092800 | bytes 4980740 | tf_op jit(solution)/shard_map/while/body/eval_jaxpr/yxz,ysz->xs/dot_general | solution.py:28
  198.3 5.2 %gather_fusion = bf16[12,256,256]{2,1,0:T(8,128)(2,1)S(1)} fusion(bf16[96,256,256]{2,1,0:T(8,128)(2,1)} %get-tuple-element.119, s32[1024]{0:T(1024)S(1)} %pad_clamp_fusion.3), kind=kCustom, calls=%fused_computation.clone.1 | custom fusion | bytes 3145776 | tf_op jit(solution)/shard_map/while/body/eval_jaxpr/gather | solution.py:24
  203.5 3.4 %fusion.27 = f32[6,256,256]{2,1,0:T(8,128)} fusion(f32[6,256,256]{2,1,0:T(8,128)} %get-tuple-element.110, s32[]{:T(128)S(6)} %copy.38, bf16[12,256,256]{2,1,0:T(8,128)(2,1)} %get-tuple-element.121, bf16[12,256,256]{2,1,0:T(8,128)(2,1)S(1)} %gather_fusion, bf16[12,256,256]{2,1,0:T(8,128)(2,1)S(1)} %get-tuple-element.120), kind=kOutput, calls=%fused_computation.6.clone.1 | convolution fusion | flops 806092800 | bytes 4980740 | tf_op jit(solution)/shard_map/while/body/eval_jaxpr/yxz,ysz->xs/dot_general | solution.py:28
  206.9 5.2 %gather_fusion = bf16[12,256,256]{2,1,0:T(8,128)(2,1)S(1)} fusion(bf16[96,256,256]{2,1,0:T(8,128)(2,1)} %get-tuple-element.119, s32[1024]{0:T(1024)S(1)} %pad_clamp_fusion.3), kind=kCustom, calls=%fused_computation.clone.1 | custom fusion | bytes 3145776 | tf_op jit(solution)/shard_map/while/body/eval_jaxpr/gather | solution.py:24
  212.2 3.4 %fusion.27 = f32[6,256,256]{2,1,0:T(8,128)} fusion(f32[6,256,256]{2,1,0:T(8,128)} %get-tuple-element.110, s32[]{:T(128)S(6)} %copy.38, bf16[12,256,256]{2,1,0:T(8,128)(2,1)} %get-tuple-element.121, bf16[12,256,256]{2,1,0:T(8,128)(2,1)S(1)} %gather_fusion, bf16[12,256,256]{2,1,0:T(8,128)(2,1)S(1)} %get-tuple-element.120), kind=kOutput, calls=%fused_computation.6.clone.1 | convolution fusion | flops 806092800 | bytes 4980740 | tf_op jit(solution)/shard_map/while/body/eval_jaxpr/yxz,ysz->xs/dot_general | solution.py:28
  215.6 0.7 dynamic-slice_bitcast_fusion
  216.4 0.3 convolution_bitcast_fusion
  216.6 0.2 dynamic-update-slice
  216.8 103.2 %all-reduce = f32[2048]{0:T(1024)S(1)} all-reduce(f32[2048]{0:T(1024)S(1)} %dynamic-update-slice), channel_id=2, replica_groups=mesh['term'=32,'sector'=16] {'term','sector'}, use_global_device_ids=true, to_apply=%add | all-reduce | flops 2048 | bytes 16384
  320.0 0.3 reshape.48
  320.6 1.4 bitcast_add_fusion
  (37 shorter events, 0.9 us)
Async XLA Ops:
  7.2 209.2 %copy-start = (bf16[4,6,8,256]{3,2,1,0:T(8,128)(2,1)S(1)}, bf16[4,6,8,256]{3,2,1,0:T(8,128)(2,1)}, u32[]{:S(2)}) copy-start(bf16[4,6,8,256]{3,2,1,0:T(8,128)(2,1)} %param.14) | copy-start | bytes 294916
  7.2 2.5 copy-start.1
  7.2 156.3 %all-gather.3.cloned.1.call-start = ((), (), s32[]{:S(2)}) async-start(), calls=%async_computation.1 | async-start | bytes 13369344 | tf_op jit(solution)/shard_map/all_gather | solution.py:20
  7.9 312.7 %reduce-scatter.2.cloned.1.call-start = ((), (), s32[]{:S(2)}) async-start(), calls=%async_computation.2 | async-start | bytes 1622016 | tf_op jit(solution)/shard_map/reduce_scatter | solution.py:36
  9.7 153.9 %copy-start.2 = (bf16[12,256,256]{2,1,0:T(8,128)(2,1)S(1)}, bf16[12,256,256]{2,1,0:T(8,128)(2,1)}, u32[]{:S(2)}) copy-start(bf16[12,256,256]{2,1,0:T(8,128)(2,1)} %param.10) | copy-start | bytes 4718596
  215.6 104.8 %copy-start.3 = (f32[4]{0:T(128)S(1)}, f32[4]{0:T(128)}, u32[]{:S(2)}) copy-start(f32[4]{0:T(128)} %param.15) | copy-start | bytes 52
  320.4 1.7 copy-start.4
Sparse Core Ops, SparseCore 0:
  10.1 153.3 all-gather.2
  215.7 97.5 reduce-scatter.1
